TPU v7x, 256 devices: a whole 4x4x8 slice. The times are simulated.
256 devices in a mesh: span: 64 (over x, z, core), mp: 4 (over y).
Axes of the slice: x: 4, y: 4, z: 8, core: 2. Of those that a mesh axis runs over, the one named last changes fastest.
Arguments:
- queries: bfloat16 [32768, 4096], P('span', 'mp'), may hold values from -6 to 6
- grad_out: bfloat16 [32768, 4096], P('span', 'mp'), may hold values from -0.59765625 to 0.59765625
- read_kv: bfloat16 [64, 896, 2, 1024], P('span', None, None, 'mp'), may hold values from -6 to 6
- read_ids: int32 [64, 28], P('span'), may hold values from 0 to 63, all different within a row
- read_counts: int32 [64, 28], P('span'), may hold values from 1 to 512
- gist_states: bfloat16 [2048, 4096], P('span'), may hold values from -16 to 16
- kv_weight: bfloat16 [4096, 2, 1024], P(None, None, 'mp'), may hold values from -0.09375 to 0.09375
Outputs:
- query_grad: bfloat16 [32768, 4096], P('span', 'mp')
- kv_weight_grad: float32 [4096, 2, 1024], P('span', None, 'mp')
- gist_state_grad: bfloat16 [2048, 4096], P('span', 'mp')
Inputs may be any that keep to these rules, and one draw needn't show every extreme that they name: `read_ids`: each span reads 28 different spans; every span is read by some span.
All inputs are finite; a program needn't handle non-finite values.
Results may differ from a plain program's by a relative error of at most 0.019.
Values may be sent and summed in bfloat16 or wider, within the bound.
A program may use at most 128 MiB of HBM per device.

v0:
```python
import jax
import jax.numpy as jnp
from jax import lax
from jax.sharding import PartitionSpec as P

HD = 128


def span_backward(query_rows, grad_rows, kv_rows, count_row, groups, gist):
    length = query_rows.shape[0]
    key_rows = kv_rows.shape[0]
    kv_width = kv_rows.shape[2]
    kv_heads = kv_width // HD
    scale = HD ** (-0.5)
    query = query_rows.reshape(length, kv_heads, groups, HD)
    upstream = grad_rows.reshape(length, kv_heads, groups, HD)
    keys = kv_rows[:, 0, :].reshape(key_rows, kv_heads, HD)
    values = kv_rows[:, 1, :].reshape(key_rows, kv_heads, HD)
    scores = (
        jnp.einsum("ikgd,jkd->kgij", query, keys, preferred_element_type=jnp.float32) * scale - 1.0
    )
    limits = length - jnp.repeat(count_row, gist)
    visible = jnp.arange(length, dtype=jnp.int32)[:, None] >= limits[None, :]
    sig = jax.nn.sigmoid(scores)
    probs = jnp.where(visible, sig, 0.0).astype(jnp.bfloat16)
    value_part = jnp.einsum("kgij,ikgd->jkd", probs, upstream, preferred_element_type=jnp.float32)
    dprob = jnp.einsum("ikgd,jkd->kgij", upstream, values, preferred_element_type=jnp.float32)
    dscore = jnp.where(visible, dprob * sig * (1.0 - sig) * scale, 0.0).astype(jnp.bfloat16)
    key_part = jnp.einsum("kgij,ikgd->jkd", dscore, query, preferred_element_type=jnp.float32)
    query_grad = jnp.einsum("kgij,jkd->ikgd", dscore, keys, preferred_element_type=jnp.float32)
    query_grad = query_grad.astype(jnp.bfloat16).reshape(length, kv_heads * groups * HD)
    parts = jnp.stack(
        [key_part.reshape(key_rows, kv_width), value_part.reshape(key_rows, kv_width)], axis=1
    )
    return (query_grad, parts)


def body(queries, grad_out, read_kv, read_ids, read_counts, gist_states, kv_weight):
    owners = lax.axis_size("span")
    local_spans = read_ids.shape[0]
    slots = read_ids.shape[1]
    kv_width = read_kv.shape[3]
    groups = queries.shape[1] // HD // (kv_width // HD)
    gist = read_kv.shape[1] // slots
    length = queries.shape[0] // local_spans
    all_spans = owners * local_spans
    query_blocks = queries.reshape(local_spans, length, queries.shape[1])
    grad_blocks = grad_out.reshape(local_spans, length, grad_out.shape[1])

    def one_span(items):
        return span_backward(items[0], items[1], items[2], items[3], groups, gist)

    query_grad, parts = lax.map(one_span, (query_blocks, grad_blocks, read_kv, read_counts))
    flat_parts = parts.reshape(local_spans * slots, gist * 2 * kv_width)
    selector = (
        read_ids.reshape(-1)[:, None] == jnp.arange(all_spans, dtype=jnp.int32)[None, :]
    ).astype(jnp.float32)
    table = lax.dot_general(
        selector,
        flat_parts,
        (((0,), (0,)), ((), ())),
        precision=lax.Precision.HIGHEST,
        preferred_element_type=jnp.float32,
    )
    table = table.reshape(owners, local_spans * gist, 2, kv_width)
    received = lax.all_to_all(
        table.astype(jnp.bfloat16), "span", split_axis=0, concat_axis=0, tiled=True
    ).astype(table.dtype)
    gist_grad = (
        jnp.sum(received, axis=0).astype(jnp.bfloat16).reshape(local_spans * gist, 2 * kv_width)
    )
    width = gist_states.shape[1]
    partial_states = jnp.dot(
        gist_grad, kv_weight.reshape(width, 2 * kv_width).T, preferred_element_type=jnp.float32
    )
    state_grad = lax.psum_scatter(
        partial_states.astype(jnp.bfloat16), "mp", scatter_dimension=1, tiled=True
    )
    my_rows = width // owners
    weight_grad = lax.psum_scatter(
        lax.dot_general(
            gist_states, gist_grad, (((0,), (0,)), ((), ())), preferred_element_type=jnp.float32
        ),
        "span",
        scatter_dimension=0,
        tiled=True,
    )
    weight_grad = weight_grad.reshape(my_rows, 2, kv_width)
    return (query_grad.reshape(local_spans * length, queries.shape[1]), weight_grad, state_grad)


def solution(mesh):
    placed = (
        P("span", "mp"),
        P("span", "mp"),
        P("span", None, None, "mp"),
        P("span", None),
        P("span", None),
        P("span", None),
        P(None, None, "mp"),
    )
    return jax.shard_map(
        body,
        mesh=mesh,
        in_specs=placed,
        out_specs=(P("span", "mp"), P("span", None, "mp"), P("span", "mp")),
        check_vma=False,
    )
```

profile of v0, /device:TPU:1, one launch (start us, length us, event | category | flops | bytes accessed | tf_op | source)
XLA Modules:
  0.0 308.8 jit_solution(634252806563158867)
XLA Ops:
  7.2 0.0 copy-start
  7.2 0.0 copy-start.6
  7.2 0.0 reduce-scatter.7.cloned.1.call-start
  7.2 2.6 copy.32
  9.8 0.1 fusion.18
  9.9 0.0 copy-start.3
  9.9 1.7 copy.60
  11.6 1.5 copy.59
  13.1 0.0 copy-done.6
  13.1 0.1 broadcast_in_dim.29
  13.2 0.1 sub.25
  13.3 0.3 iota_compare_fusion
  13.5 4.3 %add_divide_fusion = f32[2,512,4,896]{3,1,2,0:T(8,128)S(1)} fusion(bf16[512,2,4,128]{0,3,2,1:T(8,128)(2,1)S(1)} %bitcast.68, bf16[896,2,128,1]{0,2,3,1:T(8,128)(2,1)S(1)} %bitcast.77), kind=kOutput, calls=%fused_computation.2 | convolution fusion | flops 957874176 | bytes 16187392 | tf_op jit(solution)/shard_map/while/body/eval_jaxpr/ikgd,jkd->kgij/dot_general | solution.py:20
  17.8 0.0 copy-done.3
  17.9 0.0 copy-start.2
  17.9 3.2 %fusion.1 = f32[2,896,128,1]{1,2,3,0:T(8,128)} fusion(bf16[512,2,4,128]{0,3,2,1:T(8,128)(2,1)S(1)} %bitcast.72, f32[2,512,4,896]{3,1,2,0:T(8,128)S(1)} %add_divide_fusion, pred[512,896]{1,0:T(8,128)(4,1)S(1)} %iota_compare_fusion), kind=kOutput, calls=%fused_computation.4 | convolution fusion | flops 943194112 | bytes 17104896 | tf_op jit(solution)/shard_map/while/body/eval_jaxpr/kgij,ikgd->jkd/dot_general | solution.py:26
  21.1 2.2 copy-done.2
  23.3 7.1 %fusion.3 = bf16[2,4,512,896]{3,2,1,0:T(8,128)(2,1)S(1)} fusion(f32[2,512,4,896]{3,1,2,0:T(8,128)} %copy-done.2, pred[512,896]{1,0:T(8,128)(4,1)S(1)} %iota_compare_fusion, bf16[512,2,4,128]{0,3,2,1:T(8,128)(2,1)S(1)} %bitcast.73, bf16[896,2,128,1]{0,2,3,1:T(8,128)(2,1)S(1)} %bitcast.80), kind=kOutput, calls=%fused_computation.5 | convolution fusion | flops 961544192 | bytes 23986176 | tf_op jit(solution)/shard_map/while/body/eval_jaxpr/ikgd,jkd->kgij/dot_general | solution.py:27
  30.5 0.0 copy-start.1
  30.5 1.3 fusion.19
  31.7 1.7 copy-done.1
  33.4 0.0 copy-start.5
  33.4 1.1 copy.39
  34.6 3.5 %copy.40 = f32[896,1,256]{2,1,0:T(1,128)} copy(f32[896,1,256]{0,2,1:T(8,128)} %bitcast.76) | data formatting | bytes 1835008 | tf_op jit(solution)/shard_map/while/body/eval_jaxpr/stack;while/body/eval_jaxpr/reshape | solution.py:32
  38.1 2.8 pad_maximum_fusion
  40.9 2.8 reshape.67
  43.7 2.8 dot_general.41
  46.6 0.0 copy-done.5
  46.6 3.1 fusion.10
  49.6 2.2 copy.42
  51.8 64.0 %all_to_all.5 = bf16[64,32,2,256]{3,2,1,0:T(2,128)(2,1)S(1)} all-to-all(bf16[64,32,2,256]{3,2,1,0:T(2,128)(2,1)S(1)} %copy.42), channel_id=1, replica_groups=mesh['span'=64,'mp'=4] {'span'}, dimensions={0} | all-to-all | bytes 4194304 | tf_op jit(solution)/shard_map/all_to_all | solution.py:66
  115.8 1.9 reduce_sum.12
  117.7 0.0 copy-done
  117.8 4.5 %convolution_bitcast_fusion = f32[4096,512]{0,1:T(8,128)} fusion(bf16[32,512]{1,0:T(8,128)(2,1)S(1)} %bitcast.82, bf16[32,4096]{1,0:T(8,128)(2,1)S(1)} %copy-done), kind=kOutput, calls=%fused_computation.8 | convolution fusion | flops 134217728 | bytes 8683520 | tf_op jit(solution)/shard_map/dot_general | solution.py:81
  122.2 9.0 %copy.57 = f32[4096,512]{1,0:T(8,128)} copy(f32[4096,512]{0,1:T(8,128)} %convolution_bitcast_fusion) | data formatting | bytes 16777216
  131.3 0.0 copy-start.4
  131.3 0.0 reduce-scatter.7.cloned.1.call-update
  131.3 0.3 reduce-scatter.5.cloned.1.call-start
  131.6 4.3 %fusion.6 = bf16[32,4096]{1,0:T(8,128)(2,1)} fusion(bf16[4096,2,256]{2,1,0:T(2,128)(2,1)} %param.13, bf16[32,2,256]{2,1,0:T(2,128)(2,1)S(1)} %reduce_sum.12), kind=kOutput, calls=%fused_computation.10 | convolution fusion | flops 134348800 | bytes 4489216 | tf_op jit(solution)/shard_map/dot_general | solution.py:73
  135.8 0.0 reduce-scatter.5.cloned.1.call-update
  135.9 0.0 copy-done.4
  135.9 5.5 %convolution_convert_fusion = bf16[2,4,512,128]{2,3,1,0:T(8,128)(2,1)S(1)} fusion(bf16[2,4,512,896]{3,2,1,0:T(8,128)(2,1)} %copy-done.1, bf16[896,2,128,1]{0,2,3,1:T(8,128)(2,1)S(1)} %bitcast.78), kind=kOutput, calls=%fused_computation.17 | convolution fusion | flops 940048384 | bytes 8847360 | tf_op jit(solution)/shard_map/while/body/eval_jaxpr/kgij,jkd->ikgd/dot_general | solution.py:30
  141.4 1.3 copy.45
  142.7 132.0 %reduce-scatter.7.cloned.1.call-done = f32[64,512]{1,0:T(8,128)} async-done(((f32[4096,512]{1,0:T(8,128)}), f32[64,512]{1,0:T(8,128)}) %reduce-scatter.7.cloned.1.call-update) | async-done | bytes 131088
  274.7 1.0 copy.58
  275.8 0.8 copy.46
  276.5 25.4 %reduce-scatter.5.cloned.1.call-done = bf16[32,1024]{1,0:T(8,128)(2,1)} async-done(((bf16[32,4096]{1,0:T(8,128)(2,1)}), bf16[32,1024]{1,0:T(8,128)(2,1)}) %reduce-scatter.5.cloned.1.call-update) | async-done | bytes 65552 | tf_op jit(solution)/shard_map/reduce_scatter | solution.py:76
  (2 shorter events, 0.0 us)
Async XLA Ops:
  7.2 110.6 %copy-start = (bf16[32,4096]{1,0:T(8,128)(2,1)S(1)}, bf16[32,4096]{1,0:T(8,128)(2,1)}, u32[]{:S(2)}) copy-start(bf16[32,4096]{1,0:T(8,128)(2,1)} %param.12) | copy-start | bytes 786436
  7.2 5.9 %copy-start.6 = (s32[1,28]{1,0:T(1,128)S(1)}, s32[1,28]{1,0:T(1,128)}, u32[]{:S(2)}) copy-start(s32[1,28]{1,0:T(1,128)} %param.11) | copy-start | bytes 340
  7.2 267.5 %reduce-scatter.7.cloned.1.call-start = ((), (), s32[]{:S(2)}) async-start(), calls=%async_computation.4 | async-start | bytes 8519680
  9.9 7.9 %copy-start.3 = (bf16[896,1,256]{0,2,1:T(8,128)(2,1)}, bf16[896,1,256]{0,2,1:T(8,128)(2,1)S(1)}, u32[]{:S(2)}) copy-start(bf16[896,1,256]{0,2,1:T(8,128)(2,1)S(1)} %get-tuple-element.34) | copy-start | bytes 1376260
  17.9 5.5 %copy-start.2 = (f32[2,512,4,896]{3,1,2,0:T(8,128)}, f32[2,512,4,896]{3,1,2,0:T(8,128)S(1)}, u32[]{:S(2)}) copy-start(f32[2,512,4,896]{3,1,2,0:T(8,128)S(1)} %add_divide_fusion) | copy-start | bytes 44040196
  30.5 2.9 copy-start.1
  33.4 13.2 %copy-start.5 = (s32[1,28]{1,0:T(1,128)S(1)}, s32[1,28]{1,0:T(1,128)}, u32[]{:S(2)}) copy-start(s32[1,28]{1,0:T(1,128)} %param.10) | copy-start | bytes 340
  131.3 4.6 %copy-start.4 = (bf16[896,1,256]{0,2,1:T(8,128)(2,1)S(1)}, bf16[896,1,256]{0,2,1:T(8,128)(2,1)}, u32[]{:S(2)}) copy-start(bf16[896,1,256]{0,2,1:T(8,128)(2,1)} %copy-done.3) | copy-start | bytes 1376260
  131.3 170.7 %reduce-scatter.5.cloned.1.call-start = ((), (), s32[]{:S(2)}) async-start(), calls=%async_computation.3 | async-start | bytes 327680 | tf_op jit(solution)/shard_map/reduce_scatter | solution.py:76
Sparse Core Ops, SparseCore 0:
  131.4 143.2 reduce-scatter.6
  278.0 23.9 reduce-scatter.4
where the time goes:
time: 311 us; the launch traced here: 309 us
  waiting for transfers between devices  157 us (50%)
  blocking collectives  64 us (21%)
  local copies, waits for them, and re-layouts  34.5 us (11%)
  matrix products  33.3 us (11%)
  between operations  14.2 us (5%)
  other arithmetic  5.03 us (2%)
    unnamed x3, waiting for transfers between devices  132 us
    all_to_all x1, blocking collectives, body(): lax.all_to_all(table.astype(jnp.bfloat16), 'span', split_axis=0, concat_a...  64 us
    reduce_scatter x1, waiting for transfers between devices, body(): lax.psum_scatter(partial_states.astype(jnp.bfloat16), 'mp', scatter_dimen...  25.4 us
    unnamed x20, local copies, waits for them, and re-layouts  18.6 us
    dot_general x1, matrix products, span_backward(): jnp.einsum('ikgd,jkd->kgij', upstream, values, preferred_element_type=jnp...  7.12 us
  transfers between devices with their start and end apart: 2, of which 2 were waited for; matrix products, arithmetic and copies ran while one was open for 4% of the time, Pallas kernels for 0%

commit v1 on v0

v1 whole, which is shorter than its diff:
```python
import jax
import jax.numpy as jnp
from jax import lax
from jax.experimental import pallas as pl
from jax.experimental.pallas import tpu as pltpu
from jax.sharding import PartitionSpec as P

HD = 128
SLOTS = 28
G = 32
LEN = 512
ROWS = SLOTS * G
NX, NZ, NY = 4, 8, 4
TILE = 128
SCALE = HD ** (-0.5)
NT = (((1,), (1,)), ((), ()))
NN = (((1,), (0,)), ((), ()))
MESH = pl.DeviceIdType.MESH
F32, BF16 = jnp.float32, jnp.bfloat16


def dot(a, b, dims=NN):
    return lax.dot_general(a, b, dims, preferred_element_type=F32)


def unmix():
    r = lax.broadcasted_iota(jnp.int32, (256, 256), 0)
    c = lax.broadcasted_iota(jnp.int32, (256, 256), 1)
    return jnp.where(c == jnp.where(r < 128, 2 * r, 2 * r - 255), 1.0, 0.0).astype(BF16)


GS = 0
Y = 7
BASE, PER = 10, 28
CORE, XA, XB, XC, ZR, AG, WC, WX = 0, 4, 6, 8, 10, 17, 24, 25
NREMOTE = BASE + 2 * PER


def kernel(
    pos, cnt, q_hbm, do_hbm, kv_hbm, gs_hbm, w_hbm,
    dq_hbm, wg_ref, sg_ref,
    q_ref, do_ref, kv_ref, gs_ref, w_ref, dq_ref,
    k_s, v_s, kt_s, dk_s, dv_s, ds_s,
    parts, sbuf, rbuf, xs, relay, xr, pz, zr, gg, ggall,
    gsend, gsall, gst, wd, usend, ur, wp, wsend, wr, qsend, qr,
    lsem, ssem, rsem,
):
    span = lax.axis_index("span")
    y = lax.axis_index("mp")
    x, z, c = span // (NZ * 2), (span // 2) % NZ, span % 2

    def at(dx=0, dz=0, dc=0, dy=0):
        place = (((x + dx) % NX) * NZ + (z + dz) % NZ) * 2 + (c + dc) % 2
        return {"span": place, "mp": (y + dy) % NY}

    def remote(src, dst, k, to):
        return pltpu.make_async_remote_copy(
            src_ref=src, dst_ref=dst, send_sem=ssem.at[k], recv_sem=rsem.at[k],
            device_id=to, device_id_type=MESH,
        )

    loads = [pltpu.make_async_copy(kv_hbm.reshape(2 * ROWS, 256), kv_ref, lsem.at[0])]
    for n, (i, o) in enumerate(((q_hbm, q_ref), (do_hbm, do_ref))):
        loads.append(pltpu.make_async_copy(i, o, lsem.at[1 + n]))
    loads.append(pltpu.make_async_copy(gs_hbm, gs_ref, lsem.at[3]))
    loads.append(pltpu.make_async_copy(w_hbm.reshape(8192, 256), w_ref, lsem.at[4]))
    for load in loads:
        load.start()

    peers = [at(dc=1)] + [at(dx=d) for d in (1, 2, 3)]
    peers += [at(dz=d) for d in range(1, NZ)] + [at(dy=d) for d in (1, 2, 3)]
    barrier = pltpu.get_barrier_semaphore()
    for peer in peers:
        pl.semaphore_signal(barrier, inc=1, device_id=peer, device_id_type=MESH)

    lane8 = lax.broadcasted_iota(jnp.int32, (8, 128), 1)
    for h in range(2):
        parts[h, SLOTS] = jnp.zeros((G, 256), BF16)
    dk_s[...] = jnp.zeros_like(dk_s)
    dv_s[...] = jnp.zeros_like(dv_s)

    loads[0].wait()
    pm = unmix()
    for b in range(7):
        blk = dot(pm, kv_ref[b * 256 : (b + 1) * 256, :]).astype(BF16)
        for h in range(2):
            kk = blk[:128, h * 128 : (h + 1) * 128]
            k_s[h, b * 128 : (b + 1) * 128, :] = kk
            v_s[h, b * 128 : (b + 1) * 128, :] = blk[128:, h * 128 : (h + 1) * 128]
            kt_s[h, :, b * 128 : (b + 1) * 128] = kk.T

    loads[3].wait()
    for zt in range(NZ):
        for xt in range(NX):
            col = (xt * NZ + zt) * 128
            gsend[zt, :, xt * 128 : (xt + 1) * 128] = gs_ref[:, col : col + 128]
    gsall[pl.ds(pl.multiple_of(z * G, G), G), :] = gsend[z]
    pl.semaphore_wait(barrier, len(peers))

    def gs_copy(d):
        rows = pl.ds(pl.multiple_of(z * G, G), G)
        return remote(gsend.at[(z + d) % NZ], gsall.at[rows], GS + d - 1, at(dz=d))

    for d in (4, 3, 5, 2, 6, 1, 7):
        gs_copy(d).start()
    loads[1].wait()
    loads[2].wait()

    def tile_rows(ref, h, t):
        tok = pl.ds(pl.multiple_of(t * TILE, TILE), TILE)
        return jnp.concatenate(
            [ref[tok, pl.ds(pl.multiple_of(h * 512 + g * 128, 128), 128)] for g in range(4)], axis=0
        )

    def attend(i):
        h, t = i // 4, i % 4
        qt, dt = tile_rows(q_ref, h, t), tile_rows(do_ref, h, t)
        s = dot(k_s[h], qt, NT)
        dp = dot(v_s[h], dt, NT)
        bias = []
        for j in range(SLOTS):
            first = LEN - cnt[0, j] - t * TILE
            row = jnp.where(lane8 >= first, -0.5, -1e30).astype(F32)
            bias.append(jnp.concatenate([jnp.concatenate([row] * 4, axis=1)] * 4, axis=0))
        u = jnp.tanh(s * (0.5 * SCALE) + jnp.concatenate(bias, axis=0))
        probs = (0.5 + 0.5 * u).astype(BF16)
        ds = (dp * (1.0 - u * u)).astype(BF16)
        ds_s[i] = ds
        dv_s[h] += dot(probs, dt)
        dk_s[h] += dot(ds, qt)

    def finish_dq(i):
        h, t = i // 4, i % 4
        tok = pl.ds(pl.multiple_of(t * TILE, TILE), TILE)
        dqt = dot(kt_s[h], ds_s[i]) * (0.25 * SCALE)
        for g in range(4):
            cols = pl.ds(pl.multiple_of(h * 512 + g * 128, 128), 128)
            dq_ref[tok, cols] = dqt[:, g * 128 : (g + 1) * 128].T.astype(BF16)

    def block(k):
        return pl.ds(pl.multiple_of(k * G, G), G)

    def core_copy(h, d):
        return remote(sbuf.at[h, d], rbuf.at[h, d], BASE + PER * h + CORE + d, at(dc=1))

    def core_send(h):
        parts[h, :SLOTS, :, :128] = (dk_s[h] * (0.25 * SCALE)).astype(BF16).reshape(SLOTS, G, 128)
        parts[h, :SLOTS, :, 128:] = dv_s[h].astype(BF16).reshape(SLOTS, G, 128)
        for d in (2, 1, 3, 0):
            def gather(zt, carry):
                p = pos[0, (((x + d) % NX) * NZ + zt) * 2 + 1 - c]
                sbuf[h, d, block(zt), :] = parts[h, p]
                return carry
            lax.fori_loop(0, NZ, gather, 0)
            core_copy(h, d).start()

    def pair_sum(h, d):
        core_copy(h, d).wait_recv()
        def add(zt, carry):
            p = pos[0, (((x + d) % NX) * NZ + zt) * 2 + c]
            own = parts[h, p].astype(F32)
            xs[h, d, block(zt), :] = (own + rbuf[h, d, block(zt), :].astype(F32)).astype(BF16)
            return carry
        lax.fori_loop(0, NZ, add, 0)

    LO, HI = pl.ds(0, 128), pl.ds(128, 128)

    def xa(h, n):
        rows = (LO, HI)[n]
        return remote(xs.at[h, 2, rows], relay.at[h, n], BASE + PER * h + XA + n, at(dx=(1, 3)[n]))

    def xb(h, n):
        d, rows = ((1, HI), (3, LO))[n]
        return remote(xs.at[h, d, rows], xr.at[h, n, rows], BASE + PER * h + XB + n, at(dx=d))

    def xc(h, n):
        d, rows = ((1, LO), (3, HI))[n]
        return remote(xs.at[h, d, rows], xr.at[h, n, rows], BASE + PER * h + XC + n, at(dx=d))

    def x_first(h):
        pair_sum(h, 2)
        xa(h, 0).start()
        xa(h, 1).start()
        pair_sum(h, 1)
        xb(h, 0).start()
        pair_sum(h, 3)
        xb(h, 1).start()
        pair_sum(h, 0)

    def x_second(h):
        for n in range(2):
            d, rows = ((1, slice(0, 128)), (3, slice(128, 256)))[n]
            xa(h, n).wait_recv()
            xs[h, d, rows, :] = (xs[h, d, rows, :].astype(F32) + relay[h, n].astype(F32)).astype(BF16)
            xc(h, n).start()

    def z_copy(h, d):
        return remote(pz.at[h, block((z + d) % NZ)], zr.at[h, d - 1], BASE + PER * h + ZR + d - 1, at(dz=d))

    def z_send(h):
        for n in range(2):
            xb(h, n).wait_recv()
            xc(h, n).wait_recv()
        pz[h] = (xs[h, 0].astype(F32) + xr[h, 0].astype(F32) + xr[h, 1].astype(F32)).astype(BF16)
        for d in (4, 3, 5, 2, 6, 1, 7):
            z_copy(h, d).start()

    def ag_copy(h, d):
        return remote(gg.at[h], ggall.at[h, block(z)], BASE + PER * h + AG + d - 1, at(dz=d))

    def z_sum(h):
        total = pz[h, block(z), :].astype(F32)
        for d in range(1, NZ):
            z_copy(h, d).wait_recv()
            total += zr[h, d - 1].astype(F32)
        gg[h] = total.astype(BF16)
        for d in (4, 3, 5, 2, 6, 1, 7):
            ag_copy(h, d).start()
        ggall[h, block(z), :] = gg[h]

    def wc_copy(h):
        return remote(wsend.at[h], wr.at[h], BASE + PER * h + WC, at(dc=1))

    def wx_copy(h, d):
        return remote(qsend.at[h, d - 1], qr.at[h, d - 1], BASE + PER * h + WX + d - 1, at(dx=d))

    def rows_of(xt, cc):
        return pl.ds(pl.multiple_of(xt * 128 + cc * 64, 64), 64)

    def w_first(h):
        for d in range(1, NZ):
            ag_copy(h, d).wait_recv()
        wp[h] = dot(gst[...], ggall[h])
        for xt in range(NX):
            wsend[h, xt] = wp[h, rows_of(xt, 1 - c), :].astype(BF16)
        wc_copy(h).start()

    def w_second(h):
        wc_copy(h).wait_recv()
        for d in (2, 1, 3):
            xt = (x + d) % NX
            qsend[h, d - 1] = (wp[h, rows_of(xt, c), :] + wr[h, xt].astype(F32)).astype(BF16)
            wx_copy(h, d).start()

    def w_last(h):
        total = wp[h, rows_of(x, c), :] + wr[h, x].astype(F32)
        for d in (1, 2, 3):
            wx_copy(h, d).wait_recv()
            total += qr[h, d - 1].astype(F32)
        for s in range(2):
            wg_ref[:, s, h * 128 : (h + 1) * 128] = total[:, s * 128 : (s + 1) * 128]

    def y_copy(d):
        return remote(usend.at[(y + d) % NY], ur.at[d - 1], Y + d - 1, at(dy=d))

    def state_send():
        for yt in range(NY):
            rows = slice(yt * 1024, (yt + 1) * 1024)
            part = jnp.zeros((G, 1024), F32)
            for s in range(2):
                left = jnp.concatenate([gg[h, :, s * 128 : (s + 1) * 128] for h in range(2)], axis=1)
                part += dot(left, wd[s, rows, :], NT)
            usend[yt] = part.astype(BF16)
        for d in (2, 1, 3):
            y_copy(d).start()

    def state_last():
        total = usend[y].astype(F32)
        for d in (1, 2, 3):
            y_copy(d).wait_recv()
            total += ur[d - 1].astype(F32)
        sg_ref[...] = total.astype(BF16)

    def loop(i, carry):
        attend(i)
        pl.when(i == 3)(lambda: core_send(0))
        pl.when(i == 4)(lambda: x_first(0))
        pl.when(i == 5)(lambda: x_second(0))
        pl.when(i == 6)(lambda: z_send(0))
        return carry

    lax.fori_loop(0, 8, loop, 0)

    def dq_steps(lo, hi):
        lax.fori_loop(lo, hi, lambda i, carry: (finish_dq(i), carry)[1], 0)

    core_send(1)
    z_sum(0)
    x_first(1)
    for d in range(1, NZ):
        gs_copy(d).wait_recv()
    gst[...] = gsall[...].T
    dq_steps(0, 4)
    x_second(1)
    loads[4].wait()

    def split_w(b, carry):
        blk = dot(pm, w_ref[pl.ds(pl.multiple_of(b * 256, 256), 256), :]).astype(BF16)
        rows = pl.ds(pl.multiple_of(b * 128, 128), 128)
        wd[0, rows, :] = blk[:128]
        wd[1, rows, :] = blk[128:]
        return carry

    lax.fori_loop(0, 32, split_w, 0)
    z_send(1)
    dq_steps(4, 8)
    dq_out = pltpu.make_async_copy(dq_ref, dq_hbm, lsem.at[6])
    dq_out.start()
    w_first(0)
    w_second(0)
    z_sum(1)
    state_send()
    w_last(0)
    w_first(1)
    w_second(1)
    state_last()
    w_last(1)

    dq_out.wait()
    for d in range(1, NZ):
        gs_copy(d).wait_send()
    for d in (1, 2, 3):
        y_copy(d).wait_send()
    for h in range(2):
        for d in range(4):
            core_copy(h, d).wait_send()
        for n in range(2):
            xa(h, n).wait_send()
            xb(h, n).wait_send()
            xc(h, n).wait_send()
        for d in range(1, NZ):
            z_copy(h, d).wait_send()
            ag_copy(h, d).wait_send()
        wc_copy(h).wait_send()
        for d in (1, 2, 3):
            wx_copy(h, d).wait_send()


def body(queries, grad_out, read_kv, read_ids, read_counts, gist_states, kv_weight):
    smem, vmem, anywhere = (pl.BlockSpec(memory_space=m) for m in (pltpu.SMEM, pltpu.VMEM, pl.ANY))
    scratch = [
        ((512, 1024), BF16), ((512, 1024), BF16), ((2 * ROWS, 256), BF16), ((G, 4096), BF16),
        ((8192, 256), BF16), ((512, 1024), BF16),
        ((2, ROWS, 128), BF16), ((2, ROWS, 128), BF16), ((2, 128, ROWS), BF16),
        ((2, ROWS, 128), F32), ((2, ROWS, 128), F32), ((8, ROWS, 512), BF16),
    ]
    scratch2 = [
        ((2, SLOTS + 1, G, 256), BF16), ((2, 4, 256, 256), BF16), ((2, 4, 256, 256), BF16), ((2, 4, 256, 256), BF16),
        ((2, 2, 128, 256), BF16), ((2, 2, 256, 256), BF16), ((2, 256, 256), BF16), ((2, 7, G, 256), BF16),
        ((2, G, 256), BF16), ((2, 256, 256), BF16),
        ((NZ, G, 512), BF16), ((256, 512), BF16), ((512, 256), BF16), ((2, 4096, 256), BF16),
        ((NY, G, 1024), BF16), ((3, G, 1024), BF16), ((2, 512, 256), F32), ((2, NX, 64, 256), BF16),
        ((2, NX, 64, 256), BF16), ((2, 3, 64, 256), BF16), ((2, 3, 64, 256), BF16),
    ]
    spans = jnp.arange(NX * NZ * 2, dtype=jnp.int32)
    slots = jnp.arange(SLOTS, dtype=jnp.int32)
    found = read_ids[0][None, :] == spans[:, None]
    pos = jnp.min(jnp.where(found, slots[None, :], SLOTS), axis=1)[None, :]
    return pl.pallas_call(
        kernel,
        out_shape=(
            jax.ShapeDtypeStruct((512, 1024), BF16),
            jax.ShapeDtypeStruct((64, 2, 256), F32),
            jax.ShapeDtypeStruct((G, 1024), BF16),
        ),
        in_specs=[smem, smem] + [anywhere] * 5,
        out_specs=(anywhere, vmem, vmem),
        scratch_shapes=[pltpu.VMEM(*s) for s in scratch]
        + [pltpu.VMEM(*s) for s in scratch2]
        + [pltpu.SemaphoreType.DMA((7,)), pltpu.SemaphoreType.DMA((NREMOTE,)), pltpu.SemaphoreType.DMA((NREMOTE,))],
        compiler_params=pltpu.CompilerParams(
            collective_id=0, has_side_effects=True, vmem_limit_bytes=60 * 2**20
        ),
        cost_estimate=pl.CostEstimate(flops=5_000_000_000, bytes_accessed=9_000_000, transcendentals=3_670_016),
        name="gist_backward",
    )(pos, read_counts, queries, grad_out, read_kv.reshape(ROWS, 2, 256), gist_states, kv_weight)


def solution(mesh):
    placed = (
        P("span", "mp"),
        P("span", "mp"),
        P("span", None, None, "mp"),
        P("span", None),
        P("span", None),
        P("span", None),
        P(None, None, "mp"),
    )
    return jax.shard_map(
        body,
        mesh=mesh,
        in_specs=placed,
        out_specs=(P("span", "mp"), P("span", None, "mp"), P("span", "mp")),
        check_vma=False,
    )
```

time: 311 us -> 63.9 us (0.21)
  waiting for transfers between devices: 157 us -> 0 us
  blocking collectives: 64 us -> 0 us
  Pallas kernels: 0 us -> 56.5 us
  matrix products: 33.3 us -> 0 us
  local copies, waits for them, and re-layouts: 34.5 us -> 5.3 us
  between operations: 14.2 us -> 0.64 us
  other arithmetic: 5.03 us -> 1.25 us
    unnamed x3 -> x0, waiting for transfers between devices: 132 us -> none
    all_to_all x1 -> x0, blocking collectives: 64 us -> none  [body(): lax.all_to_all(table.astype(jnp.bfloat16), 'span', split_axis=0, concat_a...]
    pallas_call x0 -> x1, Pallas kernels: none -> 56.5 us  [body(): pl.pallas_call(kernel, out_shape=(jax.ShapeDtypeStruct((512, 1024), BF16)...]
    dot_general x8 -> x0, matrix products: 33.3 us -> none  [the longest x1 7.12 us: span_backward(): jnp.einsum('ikgd,jkd->kgij', upstream, values, preferred_element_type=jnp...]
    reduce_scatter x1 -> x0, waiting for transfers between devices: 25.4 us -> none  [body(): lax.psum_scatter(partial_states.astype(jnp.bfloat16), 'mp', scatter_dimen...]
    unnamed x20 -> x3, local copies, waits for them, and re-layouts: 18.6 us -> 5.3 us
    reshape x5 -> x0, local copies, waits for them, and re-layouts: 10.6 us -> none  [the longest x2 4.65 us: span_backward(): jnp.stack([key_part.reshape(key_rows, kv_width), value_part.reshape(key_r...]
  transfers between devices with their start and end apart: 2 -> 0, of which waited for: 2 -> 0; matrix products, arithmetic and copies ran while one was open for 4% -> 0% of each run, Pallas kernels for 0% -> 0%
where the time goes in v1:
time: 63.9 us; the launch traced here: 63.7 us
  Pallas kernels  56.5 us (88%)
  local copies, waits for them, and re-layouts  5.3 us (8%)
  other arithmetic  1.25 us (2%)
  between operations  0.64 us (1%)
    pallas_call x1, Pallas kernels, body(): pl.pallas_call(kernel, out_shape=(jax.ShapeDtypeStruct((512, 1024), BF16)...  56.5 us
    unnamed x3, local copies, waits for them, and re-layouts  5.3 us

profile of v1, /device:TPU:1, one launch (start us, length us, event | category | flops | bytes accessed | tf_op | source)
XLA Modules:
  0.0 63.7 jit_solution(12788676968619042129)
XLA Ops:
  0.6 1.3 %select_reduce_fusion = s32[64]{0:T(128)} fusion(s32[28]{0:T(128)} %bitcast.4), kind=kLoop, calls=%fused_computation | loop fusion | flops 5312 | bytes 368 | tf_op jit(solution)/shard_map/reduce_min | solution.py:358
  1.9 56.5 %gist_backward.1 = (bf16[512,1024]{1,0:T(8,128)(2,1)}, f32[64,2,256]{2,1,0:T(2,128)}, bf16[32,1024]{1,0:T(8,128)(2,1)}) custom-call(s32[1,64]{1,0:T(1,128)} %bitcast.5, s32[1,28]{1,0:T(1,128)} %cnt.1, bf16[512,1024]{1,0:T(8,128)(2,1)} %q_hbm.1, bf16[512,1024]{1,0:T(8,128)(2,1)} %do_hbm.1, bf16[896,2,256]{2,1,0:T(2,128)(2,1)} %bitcast.3, ...), custom_call_target="tpu_custom_call" | custom-call | flops 5000000000 | bytes 9000000 | tf_op jit(solution)/shard_map/gist_backward/pallas_call | solution.py:359
  58.4 2.3 %copy.13 = bf16[512,1024]{1,0:T(8,128)(2,1)} copy(bf16[512,1024]{1,0:T(8,128)(2,1)} %get-tuple-element.6) | data formatting | bytes 2097152
  60.7 1.6 %copy.14 = f32[64,2,256]{2,1,0:T(2,128)} copy(f32[64,2,256]{2,1,0:T(2,128)} %get-tuple-element.7) | data formatting | bytes 262144
  62.2 1.5 %copy.15 = bf16[32,1024]{1,0:T(8,128)(2,1)} copy(bf16[32,1024]{1,0:T(8,128)(2,1)} %get-tuple-element.8) | data formatting | bytes 131072

commit v2 on v1

--- a/solution.py
+++ b/solution.py
@@ -37,10 +37,10 @@
 
 
 def kernel(
-    pos, cnt, q_hbm, do_hbm, kv_hbm, gs_hbm, w_hbm,
-    dq_hbm, wg_ref, sg_ref,
-    q_ref, do_ref, kv_ref, gs_ref, w_ref, dq_ref,
-    k_s, v_s, kt_s, dk_s, dv_s, ds_s,
+    ids, cnt, q_hbm, do_hbm, kv_hbm, gs_hbm, w_hbm,
+    dq_ref, wg_ref, sg_ref,
+    q_ref, do_ref, kv_ref, gs_ref, w_ref,
+    k_s, v_s, kt_s, dk_s, dv_s, ds_s, posv, pos,
     parts, sbuf, rbuf, xs, relay, xr, pz, zr, gg, ggall,
     gsend, gsall, gst, wd, usend, ur, wp, wsend, wr, qsend, qr,
     lsem, ssem, rsem,
@@ -59,12 +59,22 @@
             device_id=to, device_id_type=MESH,
         )
 
+    sent, got = [], []
+
+    def start(copy, *which):
+        copy(*which).start()
+        sent.append((copy, which))
+
+    def arrived(copy, *which):
+        copy(*which).wait_recv()
+        got.append((copy, which))
+
     loads = [pltpu.make_async_copy(kv_hbm.reshape(2 * ROWS, 256), kv_ref, lsem.at[0])]
     for n, (i, o) in enumerate(((q_hbm, q_ref), (do_hbm, do_ref))):
         loads.append(pltpu.make_async_copy(i, o, lsem.at[1 + n]))
     loads.append(pltpu.make_async_copy(gs_hbm, gs_ref, lsem.at[3]))
     loads.append(pltpu.make_async_copy(w_hbm.reshape(8192, 256), w_ref, lsem.at[4]))
-    for load in loads:
+    for load in loads[:4]:
         load.start()
 
     peers = [at(dc=1)] + [at(dx=d) for d in (1, 2, 3)]
@@ -74,6 +84,12 @@
         pl.semaphore_signal(barrier, inc=1, device_id=peer, device_id_type=MESH)
 
     lane8 = lax.broadcasted_iota(jnp.int32, (8, 128), 1)
+    where = jnp.full((8, 128), SLOTS, jnp.int32)
+    for t in range(SLOTS):
+        where = jnp.where(lane8 == ids[0, t], t, where)
+    posv[...] = where
+    to_smem = pltpu.make_async_copy(posv, pos, lsem.at[5])
+    to_smem.start()
     for h in range(2):
         parts[h, SLOTS] = jnp.zeros((G, 256), BF16)
     dk_s[...] = jnp.zeros_like(dk_s)
@@ -89,20 +105,22 @@
             v_s[h, b * 128 : (b + 1) * 128, :] = blk[128:, h * 128 : (h + 1) * 128]
             kt_s[h, :, b * 128 : (b + 1) * 128] = kk.T
 
-    loads[3].wait()
-    for zt in range(NZ):
-        for xt in range(NX):
-            col = (xt * NZ + zt) * 128
-            gsend[zt, :, xt * 128 : (xt + 1) * 128] = gs_ref[:, col : col + 128]
-    gsall[pl.ds(pl.multiple_of(z * G, G), G), :] = gsend[z]
-    pl.semaphore_wait(barrier, len(peers))
-
     def gs_copy(d):
         rows = pl.ds(pl.multiple_of(z * G, G), G)
         return remote(gsend.at[(z + d) % NZ], gsall.at[rows], GS + d - 1, at(dz=d))
 
-    for d in (4, 3, 5, 2, 6, 1, 7):
-        gs_copy(d).start()
+    def gs_send():
+        loads[3].wait()
+        for zt in range(NZ):
+            for xt in range(NX):
+                col = (xt * NZ + zt) * 128
+                gsend[zt, :, xt * 128 : (xt + 1) * 128] = gs_ref[:, col : col + 128]
+        gsall[pl.ds(pl.multiple_of(z * G, G), G), :] = gsend[z]
+        pl.semaphore_wait(barrier, len(peers))
+        for d in (4, 3, 5, 2, 6, 1, 7):
+            start(gs_copy, d)
+        loads[4].start()
+
     loads[1].wait()
     loads[2].wait()
 
@@ -152,10 +170,10 @@
                 sbuf[h, d, block(zt), :] = parts[h, p]
                 return carry
             lax.fori_loop(0, NZ, gather, 0)
-            core_copy(h, d).start()
+            start(core_copy, h, d)
 
     def pair_sum(h, d):
-        core_copy(h, d).wait_recv()
+        arrived(core_copy, h, d)
         def add(zt, carry):
             p = pos[0, (((x + d) % NX) * NZ + zt) * 2 + c]
             own = parts[h, p].astype(F32)
@@ -179,31 +197,31 @@
 
     def x_first(h):
         pair_sum(h, 2)
-        xa(h, 0).start()
-        xa(h, 1).start()
+        start(xa, h, 0)
+        start(xa, h, 1)
         pair_sum(h, 1)
-        xb(h, 0).start()
+        start(xb, h, 0)
         pair_sum(h, 3)
-        xb(h, 1).start()
+        start(xb, h, 1)
         pair_sum(h, 0)
 
     def x_second(h):
         for n in range(2):
             d, rows = ((1, slice(0, 128)), (3, slice(128, 256)))[n]
-            xa(h, n).wait_recv()
+            arrived(xa, h, n)
             xs[h, d, rows, :] = (xs[h, d, rows, :].astype(F32) + relay[h, n].astype(F32)).astype(BF16)
-            xc(h, n).start()
+            start(xc, h, n)
 
     def z_copy(h, d):
         return remote(pz.at[h, block((z + d) % NZ)], zr.at[h, d - 1], BASE + PER * h + ZR + d - 1, at(dz=d))
 
     def z_send(h):
         for n in range(2):
-            xb(h, n).wait_recv()
-            xc(h, n).wait_recv()
+            arrived(xb, h, n)
+            arrived(xc, h, n)
         pz[h] = (xs[h, 0].astype(F32) + xr[h, 0].astype(F32) + xr[h, 1].astype(F32)).astype(BF16)
         for d in (4, 3, 5, 2, 6, 1, 7):
-            z_copy(h, d).start()
+            start(z_copy, h, d)
 
     def ag_copy(h, d):
         return remote(gg.at[h], ggall.at[h, block(z)], BASE + PER * h + AG + d - 1, at(dz=d))
@@ -211,11 +229,11 @@
     def z_sum(h):
         total = pz[h, block(z), :].astype(F32)
         for d in range(1, NZ):
-            z_copy(h, d).wait_recv()
+            arrived(z_copy, h, d)
             total += zr[h, d - 1].astype(F32)
         gg[h] = total.astype(BF16)
         for d in (4, 3, 5, 2, 6, 1, 7):
-            ag_copy(h, d).start()
+            start(ag_copy, h, d)
         ggall[h, block(z), :] = gg[h]
 
     def wc_copy(h):
@@ -229,23 +247,23 @@
 
     def w_first(h):
         for d in range(1, NZ):
-            ag_copy(h, d).wait_recv()
+            arrived(ag_copy, h, d)
         wp[h] = dot(gst[...], ggall[h])
         for xt in range(NX):
             wsend[h, xt] = wp[h, rows_of(xt, 1 - c), :].astype(BF16)
-        wc_copy(h).start()
+        start(wc_copy, h)
 
     def w_second(h):
-        wc_copy(h).wait_recv()
+        arrived(wc_copy, h)
         for d in (2, 1, 3):
             xt = (x + d) % NX
             qsend[h, d - 1] = (wp[h, rows_of(xt, c), :] + wr[h, xt].astype(F32)).astype(BF16)
-            wx_copy(h, d).start()
+            start(wx_copy, h, d)
 
     def w_last(h):
         total = wp[h, rows_of(x, c), :] + wr[h, x].astype(F32)
         for d in (1, 2, 3):
-            wx_copy(h, d).wait_recv()
+            arrived(wx_copy, h, d)
             total += qr[h, d - 1].astype(F32)
         for s in range(2):
             wg_ref[:, s, h * 128 : (h + 1) * 128] = total[:, s * 128 : (s + 1) * 128]
@@ -262,87 +280,103 @@
                 part += dot(left, wd[s, rows, :], NT)
             usend[yt] = part.astype(BF16)
         for d in (2, 1, 3):
-            y_copy(d).start()
+            start(y_copy, d)
 
     def state_last():
         total = usend[y].astype(F32)
         for d in (1, 2, 3):
-            y_copy(d).wait_recv()
+            arrived(y_copy, d)
             total += ur[d - 1].astype(F32)
         sg_ref[...] = total.astype(BF16)
 
+    def dq_steps(lo, hi):
+        lax.fori_loop(lo, hi, lambda i, carry: (finish_dq(i), carry)[1], 0)
+
+    def split_w(lo, hi):
+        def one(b, carry):
+            blk = dot(pm, w_ref[pl.ds(pl.multiple_of(b * 256, 256), 256), :]).astype(BF16)
+            rows = pl.ds(pl.multiple_of(b * 128, 128), 128)
+            wd[0, rows, :] = blk[:128]
+            wd[1, rows, :] = blk[128:]
+            return carry
+
+        lax.fori_loop(lo, hi, one, 0)
+
+    to_smem.wait()
+
     def loop(i, carry):
         attend(i)
-        pl.when(i == 3)(lambda: core_send(0))
-        pl.when(i == 4)(lambda: x_first(0))
-        pl.when(i == 5)(lambda: x_second(0))
-        pl.when(i == 6)(lambda: z_send(0))
+
+        @pl.when(i == 0)
+        def _():
+            gs_send()
+
+        @pl.when(i == 3)
+        def _():
+            core_send(0)
+
+        @pl.when(i == 5)
+        def _():
+            x_first(0)
+
+        @pl.when(i == 7)
+        def _():
+            core_send(1)
+            x_second(0)
+
         return carry
 
     lax.fori_loop(0, 8, loop, 0)
 
-    def dq_steps(lo, hi):
-        lax.fori_loop(lo, hi, lambda i, carry: (finish_dq(i), carry)[1], 0)
-
-    core_send(1)
+    loads[4].wait()
+    split_w(0, 8)
+    x_first(1)
+    dq_steps(0, 4)
+    z_send(0)
+    split_w(8, 16)
+    x_second(1)
+    split_w(16, 32)
+    for d in range(1, NZ):
+        arrived(gs_copy, d)
+    gst[...] = gsall[...].T
+    z_send(1)
     z_sum(0)
-    x_first(1)
-    for d in range(1, NZ):
-        gs_copy(d).wait_recv()
-    gst[...] = gsall[...].T
-    dq_steps(0, 4)
-    x_second(1)
-    loads[4].wait()
-
-    def split_w(b, carry):
-        blk = dot(pm, w_ref[pl.ds(pl.multiple_of(b * 256, 256), 256), :]).astype(BF16)
-        rows = pl.ds(pl.multiple_of(b * 128, 128), 128)
-        wd[0, rows, :] = blk[:128]
-        wd[1, rows, :] = blk[128:]
-        return carry
-
-    lax.fori_loop(0, 32, split_w, 0)
-    z_send(1)
     dq_steps(4, 8)
-    dq_out = pltpu.make_async_copy(dq_ref, dq_hbm, lsem.at[6])
-    dq_out.start()
+    z_sum(1)
+    state_send()
     w_first(0)
     w_second(0)
-    z_sum(1)
-    state_send()
+    w_first(1)
     w_last(0)
-    w_first(1)
     w_second(1)
     state_last()
     w_last(1)
 
-    dq_out.wait()
-    for d in range(1, NZ):
-        gs_copy(d).wait_send()
-    for d in (1, 2, 3):
-        y_copy(d).wait_send()
-    for h in range(2):
-        for d in range(4):
-            core_copy(h, d).wait_send()
-        for n in range(2):
-            xa(h, n).wait_send()
-            xb(h, n).wait_send()
-            xc(h, n).wait_send()
-        for d in range(1, NZ):
-            z_copy(h, d).wait_send()
-            ag_copy(h, d).wait_send()
-        wc_copy(h).wait_send()
-        for d in (1, 2, 3):
-            wx_copy(h, d).wait_send()
+    for copy, which in sent:
+        copy(*which).wait_send()
+
+
+def write_out(a, b, c, a_out, b_out, c_out, a_s, b_s, c_s, sem):
+    moves = [(a.at[pl.ds(r, 128)], a_s.at[pl.ds(r, 128)], a_out.at[pl.ds(r, 128)]) for r in range(0, 512, 128)]
+    moves += [(b, b_s, b_out), (c, c_s, c_out)]
+    reads = [pltpu.make_async_copy(i, s, sem.at[0, n]) for n, (i, s, _) in enumerate(moves)]
+    writes = [pltpu.make_async_copy(s, o, sem.at[1, n]) for n, (_, s, o) in enumerate(moves)]
+    for read in reads:
+        read.start()
+    for read, write in zip(reads, writes):
+        read.wait()
+        write.start()
+    for write in writes:
+        write.wait()
 
 
 def body(queries, grad_out, read_kv, read_ids, read_counts, gist_states, kv_weight):
     smem, vmem, anywhere = (pl.BlockSpec(memory_space=m) for m in (pltpu.SMEM, pltpu.VMEM, pl.ANY))
     scratch = [
         ((512, 1024), BF16), ((512, 1024), BF16), ((2 * ROWS, 256), BF16), ((G, 4096), BF16),
-        ((8192, 256), BF16), ((512, 1024), BF16),
+        ((8192, 256), BF16),
         ((2, ROWS, 128), BF16), ((2, ROWS, 128), BF16), ((2, 128, ROWS), BF16),
-        ((2, ROWS, 128), F32), ((2, ROWS, 128), F32), ((8, ROWS, 512), BF16),
+        ((2, ROWS, 128), F32), ((2, ROWS, 128), F32), ((8, ROWS, 512), BF16), ((8, 128), jnp.int32),
     ]
     scratch2 = [
         ((2, SLOTS + 1, G, 256), BF16), ((2, 4, 256, 256), BF16), ((2, 4, 256, 256), BF16), ((2, 4, 256, 256), BF16),
@@ -352,11 +386,7 @@
         ((NY, G, 1024), BF16), ((3, G, 1024), BF16), ((2, 512, 256), F32), ((2, NX, 64, 256), BF16),
         ((2, NX, 64, 256), BF16), ((2, 3, 64, 256), BF16), ((2, 3, 64, 256), BF16),
     ]
-    spans = jnp.arange(NX * NZ * 2, dtype=jnp.int32)
-    slots = jnp.arange(SLOTS, dtype=jnp.int32)
-    found = read_ids[0][None, :] == spans[:, None]
-    pos = jnp.min(jnp.where(found, slots[None, :], SLOTS), axis=1)[None, :]
-    return pl.pallas_call(
+    results = pl.pallas_call(
         kernel,
         out_shape=(
             jax.ShapeDtypeStruct((512, 1024), BF16),
@@ -364,8 +394,9 @@
             jax.ShapeDtypeStruct((G, 1024), BF16),
         ),
         in_specs=[smem, smem] + [anywhere] * 5,
-        out_specs=(anywhere, vmem, vmem),
+        out_specs=(vmem, vmem, vmem),
         scratch_shapes=[pltpu.VMEM(*s) for s in scratch]
+        + [pltpu.SMEM((8, 128), jnp.int32)]
         + [pltpu.VMEM(*s) for s in scratch2]
         + [pltpu.SemaphoreType.DMA((7,)), pltpu.SemaphoreType.DMA((NREMOTE,)), pltpu.SemaphoreType.DMA((NREMOTE,))],
         compiler_params=pltpu.CompilerParams(
@@ -373,7 +404,17 @@
         ),
         cost_estimate=pl.CostEstimate(flops=5_000_000_000, bytes_accessed=9_000_000, transcendentals=3_670_016),
         name="gist_backward",
-    )(pos, read_counts, queries, grad_out, read_kv.reshape(ROWS, 2, 256), gist_states, kv_weight)
+    )(read_ids, read_counts, queries, grad_out, read_kv.reshape(ROWS, 2, 256), gist_states, kv_weight)
+    return pl.pallas_call(
+        write_out,
+        out_shape=[jax.ShapeDtypeStruct(r.shape, r.dtype) for r in results],
+        in_specs=[anywhere] * 3,
+        out_specs=[anywhere] * 3,
+        scratch_shapes=[pltpu.VMEM(r.shape, r.dtype) for r in results] + [pltpu.SemaphoreType.DMA((2, 6))],
+        compiler_params=pltpu.CompilerParams(vmem_limit_bytes=62 * 2**20),
+        cost_estimate=pl.CostEstimate(flops=0, bytes_accessed=2_500_000, transcendentals=0),
+        name="write_out",
+    )(*results)
 
 
 def solution(mesh):

time: 63.9 us -> 52.3 us (0.82)
  local copies, waits for them, and re-layouts: 5.3 us -> 0 us
  Pallas kernels: 56.5 us -> 51.6 us
  other arithmetic: 1.25 us -> 0 us
    pallas_call x1, Pallas kernels: 56.5 us -> 49.5 us  [body(): pl.pallas_call(kernel, out_shape=(jax.ShapeDtypeStruct((512, 1024), BF16)...]
    unnamed x3 -> x0, local copies, waits for them, and re-layouts: 5.3 us -> none
    pallas_call x0 -> x1, Pallas kernels: none -> 2.07 us  [body(): pl.pallas_call(write_out, out_shape=[jax.ShapeDtypeStruct(r.shape, r.dtyp...]
    reduce_min x1 -> x0, other arithmetic: 1.25 us -> none  [body(): pos = jnp.min(jnp.where(found, slots[None, :], SLOTS), axis=1)[None, :]]
where the time goes in v2:
time: 52.3 us; the launch traced here: 52.2 us
  Pallas kernels  51.6 us (99%)
  between operations  0.64 us (1%)
    pallas_call x1, Pallas kernels, body(): pl.pallas_call(kernel, out_shape=(jax.ShapeDtypeStruct((512, 1024), BF16)...  49.5 us
    pallas_call x1, Pallas kernels, body(): pl.pallas_call(write_out, out_shape=[jax.ShapeDtypeStruct(r.shape, r.dtyp...  2.07 us

profile of v2, /device:TPU:1, one launch (start us, length us, event | category | flops | bytes accessed | tf_op | source)
XLA Modules:
  0.0 52.2 jit_solution(12989916966382372032)
XLA Ops:
  0.6 49.5 %gist_backward.1 = (bf16[512,1024]{1,0:T(8,128)(2,1)}, f32[64,2,256]{2,1,0:T(2,128)}, bf16[32,1024]{1,0:T(8,128)(2,1)}) custom-call(s32[1,28]{1,0:T(1,128)} %ids.1, s32[1,28]{1,0:T(1,128)} %cnt.1, bf16[512,1024]{1,0:T(8,128)(2,1)} %q_hbm.1, bf16[512,1024]{1,0:T(8,128)(2,1)} %do_hbm.1, bf16[896,2,256]{2,1,0:T(2,128)(2,1)} %bitcast.1, ...), custom_call_target="tpu_custom_call" | custom-call | flops 5000000000 | bytes 9000000 | tf_op jit(solution)/shard_map/gist_backward/pallas_call | solution.py:389
  50.1 2.1 %write_out.1 = (bf16[512,1024]{1,0:T(8,128)(2,1)}, f32[64,2,256]{2,1,0:T(2,128)}, bf16[32,1024]{1,0:T(8,128)(2,1)}) custom-call(bf16[512,1024]{1,0:T(8,128)(2,1)} %get-tuple-element.6.a, f32[64,2,256]{2,1,0:T(2,128)} %get-tuple-element.7.b, bf16[32,1024]{1,0:T(8,128)(2,1)} %get-tuple-element.8.c), custom_call_target="tpu_custom_call" | custom-call | bytes 2500000 | tf_op jit(solution)/shard_map/write_out/pallas_call | solution.py:408

commit v3 on v2

--- a/solution.py
+++ b/solution.py
@@ -11,6 +11,7 @@
 LEN = 512
 ROWS = SLOTS * G
 NX, NZ, NY = 4, 8, 4
+WIDTHS = (256, 256)
 TILE = 128
 SCALE = HD ** (-0.5)
 NT = (((1,), (1,)), ((), ()))
@@ -31,8 +32,8 @@
 
 GS = 0
 Y = 7
-BASE, PER = 10, 28
-CORE, XA, XB, XC, ZR, AG, WC, WX = 0, 4, 6, 8, 10, 17, 24, 25
+BASE, PER = 10, 31
+CORE, XA, XB, XC, ZR, AG, WX = 0, 4, 6, 8, 10, 17, 24
 NREMOTE = BASE + 2 * PER
 
 
@@ -40,9 +41,9 @@
     ids, cnt, q_hbm, do_hbm, kv_hbm, gs_hbm, w_hbm,
     dq_ref, wg_ref, sg_ref,
     q_ref, do_ref, kv_ref, gs_ref, w_ref,
-    k_s, v_s, kt_s, dk_s, dv_s, ds_s, posv, pos,
-    parts, sbuf, rbuf, xs, relay, xr, pz, zr, gg, ggall,
-    gsend, gsall, gst, wd, usend, ur, wp, wsend, wr, qsend, qr,
+    k_s, v_s, dk_s, dv_s, ds_s, first_s, posv, pos,
+    gsend, gsall, gst, wd, usend, ur,
+    parts, sbuf, rbuf, xs, relay, xr, pz, zr, gg, ggall, wp, wsend, qr,
     lsem, ssem, rsem,
 ):
     span = lax.axis_index("span")
@@ -77,7 +78,7 @@
     for load in loads[:4]:
         load.start()
 
-    peers = [at(dc=1)] + [at(dx=d) for d in (1, 2, 3)]
+    peers = [at(dx=d, dc=k) for d in range(NX) for k in range(2) if d or k]
     peers += [at(dz=d) for d in range(1, NZ)] + [at(dy=d) for d in (1, 2, 3)]
     barrier = pltpu.get_barrier_semaphore()
     for peer in peers:
@@ -90,8 +91,14 @@
     posv[...] = where
     to_smem = pltpu.make_async_copy(posv, pos, lsem.at[5])
     to_smem.start()
-    for h in range(2):
-        parts[h, SLOTS] = jnp.zeros((G, 256), BF16)
+    for p, width in enumerate(WIDTHS):
+        parts[p][SLOTS] = jnp.zeros((G, width), BF16)
+    lane = lane8
+    for b in range(7):
+        first = LEN - cnt[0, 4 * b + 3]
+        for j in (2, 1, 0):
+            first = jnp.where(lane < 32 * (j + 1), LEN - cnt[0, 4 * b + j], first)
+        first_s[:, b * 128 : (b + 1) * 128] = first
     dk_s[...] = jnp.zeros_like(dk_s)
     dv_s[...] = jnp.zeros_like(dv_s)
 
@@ -100,10 +107,8 @@
     for b in range(7):
         blk = dot(pm, kv_ref[b * 256 : (b + 1) * 256, :]).astype(BF16)
         for h in range(2):
-            kk = blk[:128, h * 128 : (h + 1) * 128]
-            k_s[h, b * 128 : (b + 1) * 128, :] = kk
+            k_s[h, b * 128 : (b + 1) * 128, :] = blk[:128, h * 128 : (h + 1) * 128]
             v_s[h, b * 128 : (b + 1) * 128, :] = blk[128:, h * 128 : (h + 1) * 128]
-            kt_s[h, :, b * 128 : (b + 1) * 128] = kk.T
 
     def gs_copy(d):
         rows = pl.ds(pl.multiple_of(z * G, G), G)
@@ -130,143 +135,139 @@
             [ref[tok, pl.ds(pl.multiple_of(h * 512 + g * 128, 128), 128)] for g in range(4)], axis=0
         )
 
+    token = lax.broadcasted_iota(jnp.int32, (TILE, ROWS), 0)
+
+    def half_tanh(h, t, qt):
+        first = jnp.concatenate([first_s[...]] * (TILE // 8), axis=0)
+        bias = jnp.where(token >= first - t * TILE, -0.5, -1e30).astype(F32)
+        return jnp.tanh(dot(qt, k_s[h], NT) * (0.5 * SCALE) + jnp.concatenate([bias] * 4, axis=0))
+
     def attend(i):
         h, t = i // 4, i % 4
         qt, dt = tile_rows(q_ref, h, t), tile_rows(do_ref, h, t)
-        s = dot(k_s[h], qt, NT)
-        dp = dot(v_s[h], dt, NT)
-        bias = []
-        for j in range(SLOTS):
-            first = LEN - cnt[0, j] - t * TILE
-            row = jnp.where(lane8 >= first, -0.5, -1e30).astype(F32)
-            bias.append(jnp.concatenate([jnp.concatenate([row] * 4, axis=1)] * 4, axis=0))
-        u = jnp.tanh(s * (0.5 * SCALE) + jnp.concatenate(bias, axis=0))
+        u = half_tanh(h, t, qt)
         probs = (0.5 + 0.5 * u).astype(BF16)
-        ds = (dp * (1.0 - u * u)).astype(BF16)
+        ds = (dot(dt, v_s[h], NT) * (1.0 - u * u)).astype(BF16)
         ds_s[i] = ds
-        dv_s[h] += dot(probs, dt)
-        dk_s[h] += dot(ds, qt)
+        dv_s[h] += dot(dt.T, probs)
+        dk_s[h] += dot(qt.T, ds)
 
     def finish_dq(i):
         h, t = i // 4, i % 4
         tok = pl.ds(pl.multiple_of(t * TILE, TILE), TILE)
-        dqt = dot(kt_s[h], ds_s[i]) * (0.25 * SCALE)
+        dq = (dot(ds_s[i], k_s[h]) * (0.25 * SCALE)).astype(BF16)
         for g in range(4):
             cols = pl.ds(pl.multiple_of(h * 512 + g * 128, 128), 128)
-            dq_ref[tok, cols] = dqt[:, g * 128 : (g + 1) * 128].T.astype(BF16)
+            dq_ref[tok, cols] = dq[g * 128 : (g + 1) * 128, :]
 
     def block(k):
         return pl.ds(pl.multiple_of(k * G, G), G)
 
-    def core_copy(h, d):
-        return remote(sbuf.at[h, d], rbuf.at[h, d], BASE + PER * h + CORE + d, at(dc=1))
-
-    def core_send(h):
-        parts[h, :SLOTS, :, :128] = (dk_s[h] * (0.25 * SCALE)).astype(BF16).reshape(SLOTS, G, 128)
-        parts[h, :SLOTS, :, 128:] = dv_s[h].astype(BF16).reshape(SLOTS, G, 128)
+    def core_copy(p, d):
+        return remote(sbuf[p].at[d], rbuf[p].at[d], BASE + PER * p + CORE + d, at(dc=1))
+
+    def core_send(p):
+        key_part = (dk_s[p] * (0.25 * SCALE)).astype(BF16).T
+        parts[p][:SLOTS, :, :128] = key_part.reshape(SLOTS, G, 128)
+        value_part = dv_s[p].astype(BF16).T
+        parts[p][:SLOTS, :, 128:] = value_part.reshape(SLOTS, G, 128)
         for d in (2, 1, 3, 0):
             def gather(zt, carry):
-                p = pos[0, (((x + d) % NX) * NZ + zt) * 2 + 1 - c]
-                sbuf[h, d, block(zt), :] = parts[h, p]
+                slot = pos[0, (((x + d) % NX) * NZ + zt) * 2 + 1 - c]
+                sbuf[p][d, block(zt), :] = parts[p][slot]
                 return carry
-            lax.fori_loop(0, NZ, gather, 0)
-            start(core_copy, h, d)
-
-    def pair_sum(h, d):
-        arrived(core_copy, h, d)
+            lax.fori_loop(0, NZ, gather, 0, unroll=True)
+            start(core_copy, p, d)
+
+    def pair_sum(p, d):
+        arrived(core_copy, p, d)
         def add(zt, carry):
-            p = pos[0, (((x + d) % NX) * NZ + zt) * 2 + c]
-            own = parts[h, p].astype(F32)
-            xs[h, d, block(zt), :] = (own + rbuf[h, d, block(zt), :].astype(F32)).astype(BF16)
+            slot = pos[0, (((x + d) % NX) * NZ + zt) * 2 + c]
+            own = parts[p][slot].astype(F32)
+            xs[p][d, block(zt), :] = (own + rbuf[p][d, block(zt), :].astype(F32)).astype(BF16)
             return carry
-        lax.fori_loop(0, NZ, add, 0)
+        lax.fori_loop(0, NZ, add, 0, unroll=True)
 
     LO, HI = pl.ds(0, 128), pl.ds(128, 128)
 
-    def xa(h, n):
+    def xa(p, n):
         rows = (LO, HI)[n]
-        return remote(xs.at[h, 2, rows], relay.at[h, n], BASE + PER * h + XA + n, at(dx=(1, 3)[n]))
-
-    def xb(h, n):
+        return remote(xs[p].at[2, rows], relay[p].at[n], BASE + PER * p + XA + n, at(dx=(1, 3)[n]))
+
+    def xb(p, n):
         d, rows = ((1, HI), (3, LO))[n]
-        return remote(xs.at[h, d, rows], xr.at[h, n, rows], BASE + PER * h + XB + n, at(dx=d))
-
-    def xc(h, n):
+        return remote(xs[p].at[d, rows], xr[p].at[n, rows], BASE + PER * p + XB + n, at(dx=d))
+
+    def xc(p, n):
         d, rows = ((1, LO), (3, HI))[n]
-        return remote(xs.at[h, d, rows], xr.at[h, n, rows], BASE + PER * h + XC + n, at(dx=d))
-
-    def x_first(h):
-        pair_sum(h, 2)
-        start(xa, h, 0)
-        start(xa, h, 1)
-        pair_sum(h, 1)
-        start(xb, h, 0)
-        pair_sum(h, 3)
-        start(xb, h, 1)
-        pair_sum(h, 0)
-
-    def x_second(h):
+        return remote(xs[p].at[d, rows], xr[p].at[n, rows], BASE + PER * p + XC + n, at(dx=d))
+
+    def x_first(p):
+        pair_sum(p, 2)
+        start(xa, p, 0)
+        start(xa, p, 1)
+        pair_sum(p, 1)
+        start(xb, p, 0)
+        pair_sum(p, 3)
+        start(xb, p, 1)
+        pair_sum(p, 0)
+
+    def x_second(p):
         for n in range(2):
             d, rows = ((1, slice(0, 128)), (3, slice(128, 256)))[n]
-            arrived(xa, h, n)
-            xs[h, d, rows, :] = (xs[h, d, rows, :].astype(F32) + relay[h, n].astype(F32)).astype(BF16)
-            start(xc, h, n)
-
-    def z_copy(h, d):
-        return remote(pz.at[h, block((z + d) % NZ)], zr.at[h, d - 1], BASE + PER * h + ZR + d - 1, at(dz=d))
-
-    def z_send(h):
+            arrived(xa, p, n)
+            xs[p][d, rows, :] = (xs[p][d, rows, :].astype(F32) + relay[p][n].astype(F32)).astype(BF16)
+            start(xc, p, n)
+
+    def z_copy(p, d):
+        return remote(pz[p].at[block((z + d) % NZ)], zr[p].at[d - 1], BASE + PER * p + ZR + d - 1, at(dz=d))
+
+    def z_send(p):
         for n in range(2):
-            arrived(xb, h, n)
-            arrived(xc, h, n)
-        pz[h] = (xs[h, 0].astype(F32) + xr[h, 0].astype(F32) + xr[h, 1].astype(F32)).astype(BF16)
+            arrived(xb, p, n)
+            arrived(xc, p, n)
+        pz[p][...] = (xs[p][0].astype(F32) + xr[p][0].astype(F32) + xr[p][1].astype(F32)).astype(BF16)
         for d in (4, 3, 5, 2, 6, 1, 7):
-            start(z_copy, h, d)
-
-    def ag_copy(h, d):
-        return remote(gg.at[h], ggall.at[h, block(z)], BASE + PER * h + AG + d - 1, at(dz=d))
-
-    def z_sum(h):
-        total = pz[h, block(z), :].astype(F32)
+            start(z_copy, p, d)
+
+    def ag_copy(p, d):
+        return remote(gg[p], ggall[p].at[block(z)], BASE + PER * p + AG + d - 1, at(dz=d))
+
+    def z_sum(p):
+        total = pz[p][block(z), :].astype(F32)
         for d in range(1, NZ):
-            arrived(z_copy, h, d)
-            total += zr[h, d - 1].astype(F32)
-        gg[h] = total.astype(BF16)
+            arrived(z_copy, p, d)
+            total += zr[p][d - 1].astype(F32)
+        gg[p][...] = total.astype(BF16)
         for d in (4, 3, 5, 2, 6, 1, 7):
-            start(ag_copy, h, d)
-        ggall[h, block(z), :] = gg[h]
-
-    def wc_copy(h):
-        return remote(wsend.at[h], wr.at[h], BASE + PER * h + WC, at(dc=1))
-
-    def wx_copy(h, d):
-        return remote(qsend.at[h, d - 1], qr.at[h, d - 1], BASE + PER * h + WX + d - 1, at(dx=d))
+            start(ag_copy, p, d)
+        ggall[p][block(z), :] = gg[p][...]
 
     def rows_of(xt, cc):
         return pl.ds(pl.multiple_of(xt * 128 + cc * 64, 64), 64)
 
-    def w_first(h):
+    def w_copy(p, d, k):
+        n = 2 * d + k - 1
+        rows = rows_of((x + d) % NX, (c + k) % 2)
+        return remote(wsend[p].at[rows], qr[p].at[n], BASE + PER * p + WX + n, at(dx=d, dc=k))
+
+    W_ORDER = ((2, 0), (2, 1), (1, 0), (3, 0), (1, 1), (3, 1), (0, 1))
+
+    def w_send(p):
         for d in range(1, NZ):
-            arrived(ag_copy, h, d)
-        wp[h] = dot(gst[...], ggall[h])
-        for xt in range(NX):
-            wsend[h, xt] = wp[h, rows_of(xt, 1 - c), :].astype(BF16)
-        start(wc_copy, h)
-
-    def w_second(h):
-        arrived(wc_copy, h)
-        for d in (2, 1, 3):
-            xt = (x + d) % NX
-            qsend[h, d - 1] = (wp[h, rows_of(xt, c), :] + wr[h, xt].astype(F32)).astype(BF16)
-            start(wx_copy, h, d)
-
-    def w_last(h):
-        total = wp[h, rows_of(x, c), :] + wr[h, x].astype(F32)
-        for d in (1, 2, 3):
-            arrived(wx_copy, h, d)
-            total += qr[h, d - 1].astype(F32)
+            arrived(ag_copy, p, d)
+        wp[p][...] = dot(gst[...], ggall[p][...])
+        wsend[p][...] = wp[p][...].astype(BF16)
+        for d, k in W_ORDER:
+            start(w_copy, p, d, k)
+
+    def w_last(p):
+        total = wp[p][rows_of(x, c), :]
+        for d, k in W_ORDER:
+            arrived(w_copy, p, d, k)
+            total += qr[p][2 * d + k - 1].astype(F32)
         for s in range(2):
-            wg_ref[:, s, h * 128 : (h + 1) * 128] = total[:, s * 128 : (s + 1) * 128]
+            wg_ref[:, s, p * 128 : (p + 1) * 128] = total[:, s * 128 : (s + 1) * 128]
 
     def y_copy(d):
         return remote(usend.at[(y + d) % NY], ur.at[d - 1], Y + d - 1, at(dy=d))
@@ -276,7 +277,7 @@
             rows = slice(yt * 1024, (yt + 1) * 1024)
             part = jnp.zeros((G, 1024), F32)
             for s in range(2):
-                left = jnp.concatenate([gg[h, :, s * 128 : (s + 1) * 128] for h in range(2)], axis=1)
+                left = jnp.concatenate([gg[p][:, s * 128 : (s + 1) * 128] for p in range(2)], axis=1)
                 part += dot(left, wd[s, rows, :], NT)
             usend[yt] = part.astype(BF16)
         for d in (2, 1, 3):
@@ -343,12 +344,10 @@
     z_sum(0)
     dq_steps(4, 8)
     z_sum(1)
+    w_send(0)
     state_send()
-    w_first(0)
-    w_second(0)
-    w_first(1)
+    w_send(1)
     w_last(0)
-    w_second(1)
     state_last()
     w_last(1)
 
@@ -373,18 +372,18 @@
 def body(queries, grad_out, read_kv, read_ids, read_counts, gist_states, kv_weight):
     smem, vmem, anywhere = (pl.BlockSpec(memory_space=m) for m in (pltpu.SMEM, pltpu.VMEM, pl.ANY))
     scratch = [
-        ((512, 1024), BF16), ((512, 1024), BF16), ((2 * ROWS, 256), BF16), ((G, 4096), BF16),
-        ((8192, 256), BF16),
-        ((2, ROWS, 128), BF16), ((2, ROWS, 128), BF16), ((2, 128, ROWS), BF16),
-        ((2, ROWS, 128), F32), ((2, ROWS, 128), F32), ((8, ROWS, 512), BF16), ((8, 128), jnp.int32),
+        ((512, 1024), BF16), ((512, 1024), BF16), ((2 * ROWS, 256), BF16), ((G, 4096), BF16), ((8192, 256), BF16),
+        ((2, ROWS, 128), BF16), ((2, ROWS, 128), BF16), ((2, 128, ROWS), F32), ((2, 128, ROWS), F32),
+        ((8, 512, ROWS), BF16), ((8, ROWS), jnp.int32), ((8, 128), jnp.int32),
     ]
     scratch2 = [
-        ((2, SLOTS + 1, G, 256), BF16), ((2, 4, 256, 256), BF16), ((2, 4, 256, 256), BF16), ((2, 4, 256, 256), BF16),
-        ((2, 2, 128, 256), BF16), ((2, 2, 256, 256), BF16), ((2, 256, 256), BF16), ((2, 7, G, 256), BF16),
-        ((2, G, 256), BF16), ((2, 256, 256), BF16),
         ((NZ, G, 512), BF16), ((256, 512), BF16), ((512, 256), BF16), ((2, 4096, 256), BF16),
-        ((NY, G, 1024), BF16), ((3, G, 1024), BF16), ((2, 512, 256), F32), ((2, NX, 64, 256), BF16),
-        ((2, NX, 64, 256), BF16), ((2, 3, 64, 256), BF16), ((2, 3, 64, 256), BF16),
+        ((NY, G, 1024), BF16), ((3, G, 1024), BF16),
+    ]
+    by_piece = [
+        ((SLOTS + 1, G), BF16), ((4, 256), BF16), ((4, 256), BF16), ((4, 256), BF16),
+        ((2, 128), BF16), ((2, 256), BF16), ((256,), BF16), ((7, G), BF16), ((G,), BF16), ((256,), BF16),
+        ((512,), F32), ((512,), BF16), ((7, 64), BF16),
     ]
     results = pl.pallas_call(
         kernel,
@@ -398,6 +397,7 @@
         scratch_shapes=[pltpu.VMEM(*s) for s in scratch]
         + [pltpu.SMEM((8, 128), jnp.int32)]
         + [pltpu.VMEM(*s) for s in scratch2]
+        + [tuple(pltpu.VMEM(shape + (w,), kind) for w in WIDTHS) for shape, kind in by_piece]
         + [pltpu.SemaphoreType.DMA((7,)), pltpu.SemaphoreType.DMA((NREMOTE,)), pltpu.SemaphoreType.DMA((NREMOTE,))],
         compiler_params=pltpu.CompilerParams(
             collective_id=0, has_side_effects=True, vmem_limit_bytes=60 * 2**20

time: 52.3 us -> 49.8 us (0.952)
  Pallas kernels: 51.6 us -> 49 us
    pallas_call x1, Pallas kernels: 49.5 us -> 46.9 us  [body(): pl.pallas_call(kernel, out_shape=(jax.ShapeDtypeStruct((512, 1024), BF16)...]
where the time goes in v3:
time: 49.8 us; the launch traced here: 49.6 us
  Pallas kernels  49 us (98%)
  between operations  0.64 us (1%)
    pallas_call x1, Pallas kernels, body(): pl.pallas_call(kernel, out_shape=(jax.ShapeDtypeStruct((512, 1024), BF16)...  46.9 us
    pallas_call x1, Pallas kernels, body(): pl.pallas_call(write_out, out_shape=[jax.ShapeDtypeStruct(r.shape, r.dtyp...  2.07 us

profile of v3, /device:TPU:1, one launch (start us, length us, event | category | flops | bytes accessed | tf_op | source)
XLA Modules:
  0.0 49.6 jit_solution(18097868995703300534)
XLA Ops:
  0.6 46.9 %gist_backward.1 = (bf16[512,1024]{1,0:T(8,128)(2,1)}, f32[64,2,256]{2,1,0:T(2,128)}, bf16[32,1024]{1,0:T(8,128)(2,1)}) custom-call(s32[1,28]{1,0:T(1,128)} %ids.1, s32[1,28]{1,0:T(1,128)} %cnt.1, bf16[512,1024]{1,0:T(8,128)(2,1)} %q_hbm.1, bf16[512,1024]{1,0:T(8,128)(2,1)} %do_hbm.1, bf16[896,2,256]{2,1,0:T(2,128)(2,1)} %bitcast.1, ...), custom_call_target="tpu_custom_call" | custom-call | flops 5000000000 | bytes 9000000 | tf_op jit(solution)/shard_map/gist_backward/pallas_call | solution.py:388
  47.6 2.1 %write_out.1 = (bf16[512,1024]{1,0:T(8,128)(2,1)}, f32[64,2,256]{2,1,0:T(2,128)}, bf16[32,1024]{1,0:T(8,128)(2,1)}) custom-call(bf16[512,1024]{1,0:T(8,128)(2,1)} %get-tuple-element.6.a, f32[64,2,256]{2,1,0:T(2,128)} %get-tuple-element.7.b, bf16[32,1024]{1,0:T(8,128)(2,1)} %get-tuple-element.8.c), custom_call_target="tpu_custom_call" | custom-call | bytes 2500000 | tf_op jit(solution)/shard_map/write_out/pallas_call | solution.py:408

commit v4 on v3

--- a/solution.py
+++ b/solution.py
@@ -308,7 +308,7 @@
     def loop(i, carry):
         attend(i)
 
-        @pl.when(i == 0)
+        @pl.when(i == 1)
         def _():
             gs_send()
 
@@ -344,8 +344,8 @@
     z_sum(0)
     dq_steps(4, 8)
     z_sum(1)
+    state_send()
     w_send(0)
-    state_send()
     w_send(1)
     w_last(0)
     state_last()

time: 49.8 us -> 50.4 us (1.012)
  Pallas kernels: 49 us -> 49.6 us
    pallas_call x1, Pallas kernels: 46.9 us -> 47.6 us  [body(): pl.pallas_call(kernel, out_shape=(jax.ShapeDtypeStruct((512, 1024), BF16)...]
where the time goes in v4:
time: 50.4 us; the launch traced here: 50.3 us
  Pallas kernels  49.6 us (98%)
  between operations  0.64 us (1%)
    pallas_call x1, Pallas kernels, body(): pl.pallas_call(kernel, out_shape=(jax.ShapeDtypeStruct((512, 1024), BF16)...  47.6 us
    pallas_call x1, Pallas kernels, body(): pl.pallas_call(write_out, out_shape=[jax.ShapeDtypeStruct(r.shape, r.dtyp...  2.07 us

profile of v4, /device:TPU:1, one launch (start us, length us, event | category | flops | bytes accessed | tf_op | source)
XLA Modules:
  0.0 50.3 jit_solution(15004068345160842153)
XLA Ops:
  0.6 47.6 %gist_backward.1 = (bf16[512,1024]{1,0:T(8,128)(2,1)}, f32[64,2,256]{2,1,0:T(2,128)}, bf16[32,1024]{1,0:T(8,128)(2,1)}) custom-call(s32[1,28]{1,0:T(1,128)} %ids.1, s32[1,28]{1,0:T(1,128)} %cnt.1, bf16[512,1024]{1,0:T(8,128)(2,1)} %q_hbm.1, bf16[512,1024]{1,0:T(8,128)(2,1)} %do_hbm.1, bf16[896,2,256]{2,1,0:T(2,128)(2,1)} %bitcast.1, ...), custom_call_target="tpu_custom_call" | custom-call | flops 5000000000 | bytes 9000000 | tf_op jit(solution)/shard_map/gist_backward/pallas_call | solution.py:388
  48.2 2.1 %write_out.1 = (bf16[512,1024]{1,0:T(8,128)(2,1)}, f32[64,2,256]{2,1,0:T(2,128)}, bf16[32,1024]{1,0:T(8,128)(2,1)}) custom-call(bf16[512,1024]{1,0:T(8,128)(2,1)} %get-tuple-element.6.a, f32[64,2,256]{2,1,0:T(2,128)} %get-tuple-element.7.b, bf16[32,1024]{1,0:T(8,128)(2,1)} %get-tuple-element.8.c), custom_call_target="tpu_custom_call" | custom-call | bytes 2500000 | tf_op jit(solution)/shard_map/write_out/pallas_call | solution.py:408
